TPU v7x, 512 devices: a whole 4x4x16 slice. The times are simulated.
512 devices in a mesh: dp: 8 (over x, core), table: 64 (over y, z).
Axes of the slice: x: 4, y: 4, z: 16, core: 2. Of those that a mesh axis runs over, the one named last changes fastest.
Arguments:
- cotangent: bfloat16 [131072, 256], P(('dp', 'table')), may hold values from -1.5 to 1.5
- hot_ids: int32 [131072, 8], P(('dp', 'table')), may hold values from 0 to 2047
- cold_owner: int32 [131072, 4], P(('dp', 'table')), may hold values from 0 to 63, all different within a row; in each aligned block of 256 rows (0 to 255, 256 to 511, ...) at most 24 rows name the same one
- cold_slot: int32 [131072, 4], P(('dp', 'table')), may hold values from 0 to 127
- live_rows: int32 [64], P('table'), may hold values from 128 to 256, as said below
- hot_weight: float32 [2048, 256], P('table'), may hold values from -0.6 to 0.6
- hot_first: float32 [2048, 256], P('table'), may hold values from -1.2 to 1.2
- hot_second: float32 [2048, 256], P('table'), may hold values from 0.001 to 0.1
- cold_weight: float32 [16384, 256], P('table'), may hold values from -0.6 to 0.6
- cold_first: float32 [16384, 256], P('table'), may hold values from -1.2 to 1.2
- cold_second: float32 [16384, 256], P('table'), may hold values from 0.001 to 0.1
Outputs:
- new_hot_weight: float32 [2048, 256], P('table')
- new_hot_first: float32 [2048, 256], P('table')
- new_hot_second: float32 [2048, 256], P('table')
- new_cold_weight: float32 [16384, 256], P('table')
- new_cold_first: float32 [16384, 256], P('table')
- new_cold_second: float32 [16384, 256], P('table')
Inputs may be any that keep to these rules, and one draw needn't show every extreme that they name: `cold_owner`: within the samples of one device (aligned blocks of 256 samples) no owner is named more than 24 times; the 4 owners of a sample differ. `cold_slot`: lookups name only the first 128 slots of a window, which lie inside every shard's live rows. `live_rows`: each count is a multiple of 64; some shard uses its whole window and some uses half.
All inputs are finite; a program needn't handle non-finite values.
Results may differ from a plain program's by a relative error of at most 0.0015.
Values may be sent and summed in bfloat16 or wider, within the bound.
A program may use at most 64 MiB of HBM per device.

v0:
```python
import math

import jax
import jax.numpy as jnp
from jax import lax
from jax.sharding import PartitionSpec as P

STEP = 3


BETA_ONE = 0.9
BETA_TWO = 0.999
ADAM_EPS = 1e-08
LEARN_RATE = 0.05
CLIP_NORM = 4.0


def adam_update(weight, moment_one, moment_two, gradient, active):
    row_norm = jnp.sqrt(jnp.sum(gradient * gradient, axis=1, keepdims=True))
    clipped = gradient * (CLIP_NORM / jnp.maximum(row_norm, CLIP_NORM))
    first_new = BETA_ONE * moment_one + (1.0 - BETA_ONE) * clipped
    second_new = BETA_TWO * moment_two + (1.0 - BETA_TWO) * clipped * clipped
    correct_one = 1.0 - BETA_ONE**STEP
    correct_two = 1.0 - BETA_TWO**STEP
    stepped = weight - LEARN_RATE * (first_new / correct_one) / (
        jnp.sqrt(second_new / correct_two) + ADAM_EPS
    )
    return (
        jnp.where(active, stepped, weight),
        jnp.where(active, first_new, moment_one),
        jnp.where(active, second_new, moment_two),
    )


def per_device(
    cotangent,
    hot_ids,
    cold_owner,
    cold_slot,
    live_rows,
    hot_weight,
    hot_first,
    hot_second,
    cold_weight,
    cold_first,
    cold_second,
):
    features = cotangent.shape[1]
    hot_local = hot_weight.shape[0]
    shards = lax.axis_size("table")

    def hot_block(first_row, block_rows):
        row_ids = first_row + lax.iota(jnp.int32, block_rows)
        matches = (hot_ids[None, :, :] == row_ids[:, None, None]).astype(jnp.int32)
        hits = jnp.sum(matches, axis=2).astype(jnp.bfloat16)
        return jnp.dot(hits, cotangent, preferred_element_type=jnp.float32)

    row_count = hot_local * shards
    block_rows = math.gcd(row_count, 512)
    firsts = block_rows * lax.iota(jnp.int32, row_count // block_rows)
    pieces = lax.map(lambda first_row: hot_block(first_row, block_rows), firsts)
    summed = lax.psum(pieces.reshape(row_count, features), ("dp", "table"))
    hot_grad = lax.dynamic_slice_in_dim(summed, lax.axis_index("table") * hot_local, hot_local, 0)
    per_sample = cold_owner.shape[1]
    owners = cold_owner.reshape(-1)
    slot_ids = cold_slot.reshape(-1)
    lookups = owners.shape[0]
    capacity = 3 * lookups // (2 * shards)
    owner_match = (owners[:, None] == lax.iota(jnp.int32, shards)[None, :]).astype(jnp.int32)
    bucket_rank = jnp.sum(jnp.cumsum(owner_match, axis=0) * owner_match, axis=1) - 1
    target = owners * capacity + bucket_rank
    lookup_rows = jnp.repeat(cotangent, per_sample, axis=0)
    outgoing = jnp.zeros((shards * capacity, features), jnp.bfloat16).at[target].set(lookup_rows)
    out_slots = jnp.full((shards * capacity,), -1, jnp.int32).at[target].set(slot_ids)
    arrived, arrived_slots = (
        lax.all_to_all(
            outgoing.reshape(shards, capacity, features),
            "table",
            split_axis=0,
            concat_axis=0,
            tiled=True,
        ),
        lax.all_to_all(
            out_slots.reshape(shards, capacity), "table", split_axis=0, concat_axis=0, tiled=True
        ),
    )
    window_rows = cold_weight.shape[0]
    placed = (lax.iota(jnp.int32, window_rows)[:, None] == arrived_slots.reshape(1, -1)).astype(
        jnp.bfloat16
    )
    local_grad = jnp.dot(placed, arrived.reshape(-1, features), preferred_element_type=jnp.float32)
    cold_grad = lax.psum(local_grad.astype(jnp.bfloat16), "dp").astype(jnp.float32)
    hot_active = jnp.ones((hot_local, 1), dtype=bool)
    cold_active = (lax.iota(jnp.int32, window_rows) < live_rows[0])[:, None]
    hot_new = adam_update(hot_weight, hot_first, hot_second, hot_grad, hot_active)
    cold_new = adam_update(cold_weight, cold_first, cold_second, cold_grad, cold_active)
    return (hot_new[0], hot_new[1], hot_new[2], cold_new[0], cold_new[1], cold_new[2])


def solution(mesh):
    in_specs = (
        P(("dp", "table"), None),
        P(("dp", "table"), None),
        P(("dp", "table"), None),
        P(("dp", "table"), None),
        P("table"),
        P("table", None),
        P("table", None),
        P("table", None),
        P("table", None),
        P("table", None),
        P("table", None),
    )
    out_specs = (
        P("table", None),
        P("table", None),
        P("table", None),
        P("table", None),
        P("table", None),
        P("table", None),
    )
    return jax.shard_map(
        per_device, mesh=mesh, in_specs=in_specs, out_specs=out_specs, check_vma=False
    )
```

profile of v0, /device:TPU:1, one launch (start us, length us, event | category | flops | bytes accessed | tf_op | source)
XLA Modules:
  0.0 666.1 jit_solution(8205886443293326305)
XLA Ops:
  8.0 0.0 copy-start.8
  8.0 0.0 copy-start
  8.0 0.7 broadcast_multiply_fusion
  8.7 0.8 copy.34
  9.6 0.1 eq.58
  9.7 0.1 eq.54
  9.8 0.1 copy.33
  9.9 0.1 mul.133
  10.1 18.0 %reduce-window.6 = s32[64,8,128]{2,1,0:T(8,128)S(1)} reduce-window(s32[64,8,128]{2,1,0:T(8,128)S(1)} %fusion.14, s32[]{:T(128)} %constant.25.clone.1), window={size=1x1x128 pad=0_0x0_0x127_0}, to_apply=%region_5.6 | reduce-window | flops 8323072 | bytes 524292 | tf_op jit(solution)/shard_map/reduce-window
  28.1 0.1 slice.8
  28.2 0.1 copy.36
  28.4 0.1 copy.37
  28.5 0.1 broadcast_add_fusion
  28.7 0.1 fusion.12
  28.7 0.0 copy-done.8
  28.8 0.1 copy.38
  28.9 0.1 reshape.120
  29.0 0.0 copy-start.4
  29.0 4.3 scatter_custom_fusion
  33.4 0.7 all_to_all.9
  34.1 19.3 %all-to-all-start = ((s32[64,1,24]{2,1,0:T(1,128)}), s32[64,1,24]{2,1,0:T(1,128)S(1)}, u32[]{:S(2)}, u32[]{:S(2)}) async-start(s32[64,1,24]{2,1,0:T(1,128)} %bitcast.8), calls=%async_computation | async-start | bytes 65536 | tf_op jit(solution)/shard_map/all_to_all | solution.py:83
  53.4 0.0 copy-done
  53.4 0.1 broadcast_in_dim.56
  53.5 0.1 reshape.128
  53.7 5.9 scatter_custom_fusion.1
  59.5 7.0 %all-to-all-done = s32[64,1,24]{2,1,0:T(1,128)S(1)} async-done(((s32[64,1,24]{2,1,0:T(1,128)}), s32[64,1,24]{2,1,0:T(1,128)S(1)}, u32[]{:S(2)}, u32[]{:S(2)}) %all-to-all-start) | async-done | bytes 6176 | tf_op jit(solution)/shard_map/all_to_all | solution.py:83
  66.6 7.5 %all-to-all-start.1 = ((bf16[64,24,256]{2,1,0:T(8,128)(2,1)}), bf16[64,24,256]{2,1,0:T(8,128)(2,1)S(1)}, u32[]{:S(2)}, u32[]{:S(2)}) async-start(bf16[64,24,256]{2,1,0:T(8,128)(2,1)} %bitcast.9), calls=%async_computation.1 | async-start | bytes 1572864 | tf_op jit(solution)/shard_map/all_to_all | solution.py:76
  74.1 0.0 all-reduce.3.cloned.1.call-start
  74.2 0.0 copy-done.4
  74.2 31.0 %while.10 = (s32[]{:T(128)}, f32[4,512,256]{2,1,0:T(8,128)}, s32[256,8]{0,1:T(8,128)S(1)}, s32[4]{0:T(128)S(1)}, bf16[256,256]{1,0:T(8,128)(2,1)S(1)}, /*index=5*/s32[]{:T(128)}) while((s32[]{:T(128)}, f32[4,512,256]{2,1,0:T(8,128)}, s32[256,8]{0,1:T(8,128)S(1)}, s32[4]{0:T(128)S(1)}, bf16[256,256]{1,0:T(8,128)(2,1)S(1)}, ...), condition=%wide.region_2.3_spmd, body=%wide.region_0.2_spmd.sunk | while | flops 70255104 | bytes 1716321 | solution.py:61
  74.2 0.6 dynamic_slice.14
  74.8 0.6 iota_add_fusion.2
  75.4 5.5 convert_reduce_fusion.2
  80.9 1.0 fusion.27
  81.9 0.6 dynamic_slice.14
  82.5 0.6 iota_add_fusion.2
  83.2 5.5 convert_reduce_fusion.2
  88.7 1.0 fusion.27
  89.7 0.6 dynamic_slice.14
  90.3 0.6 iota_add_fusion.2
  90.9 5.5 convert_reduce_fusion.2
  96.4 1.0 fusion.27
  97.4 0.6 dynamic_slice.14
  98.0 0.6 iota_add_fusion.2
  98.7 5.5 convert_reduce_fusion.2
  104.2 1.0 fusion.27
  105.2 0.0 copy-start.2
  105.2 0.0 copy-start.3
  105.2 0.0 all-reduce.3.cloned.1.call-update
  105.3 0.0 all-reduce.5.cloned.1.call-start
  106.0 0.5 broadcast.121
  106.6 0.7 reduce.3
  107.3 0.1 eq.62
  107.4 475.6 %all-reduce.3.cloned.1.call-done = f32[2048,256]{1,0:T(8,128)} async-done(((f32[2048,256]{1,0:T(8,128)}), f32[2048,256]{1,0:T(8,128)}) %all-reduce.3.cloned.1.call-update) | async-done | bytes 2097168 | tf_op jit(solution)/shard_map/psum | solution.py:62
  583.0 0.9 multiply_reduce_fusion
  583.9 0.0 all-to-all-done.1
  583.9 1.0 fusion.3
  585.0 0.0 all-reduce.5.cloned.1.call-update
  585.0 0.0 copy-done.5
  585.0 0.0 copy-done.6
  585.0 1.5 divide_subtract_fusion
  586.5 69.0 %all-reduce.5.cloned.1.call-done = bf16[256,256]{1,0:T(8,128)(2,1)} async-done(((bf16[256,256]{1,0:T(8,128)(2,1)}), bf16[256,256]{1,0:T(8,128)(2,1)}) %all-reduce.5.cloned.1.call-update) | async-done | bytes 131088 | tf_op jit(solution)/shard_map/psum | solution.py:92
  655.5 1.0 fusion.9
  656.5 2.1 fusion.15
  (18 shorter events, 0.1 us)
Async XLA Ops:
  8.0 20.7 %copy-start.8 = (s32[256,4]{0,1:T(4,128)S(1)}, s32[256,4]{0,1:T(4,128)}, u32[]{:S(2)}) copy-start(s32[256,4]{0,1:T(4,128)} %param.16) | copy-start | bytes 12292
  8.0 45.4 %copy-start = (bf16[256,256]{1,0:T(8,128)(2,1)S(1)}, bf16[256,256]{1,0:T(8,128)(2,1)}, u32[]{:S(2)}) copy-start(bf16[256,256]{1,0:T(8,128)(2,1)} %param.13) | copy-start | bytes 393220
  29.0 45.1 %copy-start.4 = (s32[256,8]{0,1:T(8,128)S(1)}, s32[256,8]{0,1:T(8,128)}, u32[]{:S(2)}) copy-start(s32[256,8]{0,1:T(8,128)} %param.14) | copy-start | bytes 24580
  34.1 32.5 %all-to-all-start = ((s32[64,1,24]{2,1,0:T(1,128)}), s32[64,1,24]{2,1,0:T(1,128)S(1)}, u32[]{:S(2)}, u32[]{:S(2)}) async-start(s32[64,1,24]{2,1,0:T(1,128)} %bitcast.8), calls=%async_computation | async-start | bytes 65536 | tf_op jit(solution)/shard_map/all_to_all | solution.py:83
  66.6 517.3 %all-to-all-start.1 = ((bf16[64,24,256]{2,1,0:T(8,128)(2,1)}), bf16[64,24,256]{2,1,0:T(8,128)(2,1)S(1)}, u32[]{:S(2)}, u32[]{:S(2)}) async-start(bf16[64,24,256]{2,1,0:T(8,128)(2,1)} %bitcast.9), calls=%async_computation.1 | async-start | bytes 1572864 | tf_op jit(solution)/shard_map/all_to_all | solution.py:76
  74.1 508.9 %all-reduce.3.cloned.1.call-start = ((), (), s32[]{:S(2)}) async-start(), calls=%async_computation.2 | async-start | bytes 4194304 | tf_op jit(solution)/shard_map/psum | solution.py:62
  105.2 479.8 %copy-start.5 = (f32[32,256]{1,0:T(8,128)S(1)}, f32[32,256]{1,0:T(8,128)}, u32[]{:S(2)}) copy-start(f32[32,256]{1,0:T(8,128)} %param.18) | copy-start | bytes 98308
  105.2 479.8 %copy-start.6 = (f32[32,256]{1,0:T(8,128)S(1)}, f32[32,256]{1,0:T(8,128)}, u32[]{:S(2)}) copy-start(f32[32,256]{1,0:T(8,128)} %param.19) | copy-start | bytes 98308
  105.2 479.8 %copy-start.7 = (f32[32,256]{1,0:T(8,128)S(1)}, f32[32,256]{1,0:T(8,128)}, u32[]{:S(2)}) copy-start(f32[32,256]{1,0:T(8,128)} %param.20) | copy-start | bytes 98308
  105.2 551.3 %copy-start.1 = (f32[256,256]{1,0:T(8,128)S(1)}, f32[256,256]{1,0:T(8,128)}, u32[]{:S(2)}) copy-start(f32[256,256]{1,0:T(8,128)} %param.23) | copy-start | bytes 786436
  105.2 551.3 %copy-start.2 = (f32[256,256]{1,0:T(8,128)S(1)}, f32[256,256]{1,0:T(8,128)}, u32[]{:S(2)}) copy-start(f32[256,256]{1,0:T(8,128)} %param.21) | copy-start | bytes 786436
  105.2 551.3 %copy-start.3 = (f32[256,256]{1,0:T(8,128)S(1)}, f32[256,256]{1,0:T(8,128)}, u32[]{:S(2)}) copy-start(f32[256,256]{1,0:T(8,128)} %param.22) | copy-start | bytes 786436
  105.3 550.2 %all-reduce.5.cloned.1.call-start = ((), (), s32[]{:S(2)}) async-start(), calls=%async_computation.3 | async-start | bytes 262144 | tf_op jit(solution)/shard_map/psum | solution.py:92
Sparse Core Ops, SparseCore 0:
  105.4 477.5 all-reduce.2
Sparse Core Ops, SparseCore 1:
  585.1 70.4 all-reduce.4
where the time goes:
time: 667 us; the launch traced here: 666 us
  waiting for transfers between devices  552 us (83%)
  other arithmetic  49.7 us (7%)
  starting transfers between devices  26.9 us (4%)
  between operations  16.5 us (2%)
  local copies, waits for them, and re-layouts  16 us (2%)
    psum x1, waiting for transfers between devices, per_device(): summed = lax.psum(pieces.reshape(row_count, features), ('dp', 'table'))  476 us
    psum x1, waiting for transfers between devices, per_device(): lax.psum(local_grad.astype(jnp.bfloat16), 'dp').astype(jnp.float32)  69 us
    reduce_sum x4, other arithmetic, hot_block(): hits = jnp.sum(matches, axis=2).astype(jnp.bfloat16)  21.9 us
    all_to_all x1, starting transfers between devices, per_device(): lax.all_to_all(out_slots.reshape(shards, capacity), 'table', split_axis=0...  19.3 us
    another operation x3, other arithmetic  18.2 us
  transfers between devices with their start and end apart: 4, of which 3 were waited for; matrix products, arithmetic and copies ran while one was open for 6% of the time, Pallas kernels for 0%

commit v1 on v0

v1 whole, which is shorter than its diff:
```python
import functools

import jax
import jax.numpy as jnp
from jax import lax
from jax.experimental import pallas as pl
from jax.experimental.pallas import tpu as pltpu
from jax.sharding import PartitionSpec as P

STEP = 3
BETA_ONE = 0.9
BETA_TWO = 0.999
ADAM_EPS = 1e-08
LEARN_RATE = 0.05
CLIP_NORM = 4.0

NX, NC, NY, NZ = 4, 2, 4, 16
SAMP = 256
FEAT = 256
HOT_LOCAL = 32
WINDOW = 256
TOUCHED = 128
NDP = NX * NC
HOT_SHARE = HOT_LOCAL // NDP
COLD_SHARE = TOUCHED // NDP
CHUNKS = 4
PER = NZ // CHUNKS
BLOCK = PER * (COLD_SHARE + HOT_SHARE)
Z_ORDER = [NZ // 2 + n // 2 if n % 2 == 0 else NZ // 2 - 1 - n // 2 for n in range(NZ)]
LOGICAL = pl.DeviceIdType.MESH


def comm_kernel(
    cot_hbm, hot_hbm, owner_hbm, slot_hbm, out,
    hot_in, owner_in, slot_in, ids, cot, slotfor, counts, psum_own, ysend, yrecv, zown, zsend, zrecv, fbuf,
    load_sem, id_send, id_recv, cot_send, fwd_send, cot_recv, y_send, y_recv, z_send, z_recv, f_send, f_recv,
):
    d = lax.axis_index("dp")
    t = lax.axis_index("table")
    x, c = d // NC, d % NC
    y, z = t // NZ, t % NZ

    def dp_peer(k, e):
        core = (1 - c) if e else c
        return (lax.rem(x + k, NX) * NC + core, t)

    def y_peer(r):
        return (d, lax.rem(y + r, NY) * NZ + z)

    def z_peer(r):
        return (d, y * NZ + lax.rem(z + r, NZ))

    dp_offsets = [(k, e) for k in range(NX) for e in range(NC) if (k, e) != (0, 0)]

    barrier = pltpu.get_barrier_semaphore()
    for r in sorted(range(1, NZ), key=lambda r: -min(r, NZ - r)):
        pl.semaphore_signal(barrier, inc=1, device_id=z_peer(r), device_id_type=LOGICAL)
    for r in range(1, NY):
        pl.semaphore_signal(barrier, inc=1, device_id=y_peer(r), device_id_type=LOGICAL)
    for k, e in dp_offsets:
        pl.semaphore_signal(barrier, inc=1, device_id=dp_peer(k, e), device_id_type=LOGICAL)

    loads = [
        pltpu.make_async_copy(hot_hbm, hot_in, load_sem.at[0]),
        pltpu.make_async_copy(owner_hbm, owner_in, load_sem.at[1]),
        pltpu.make_async_copy(slot_hbm, slot_in, load_sem.at[2]),
        pltpu.make_async_copy(cot_hbm, cot.at[0], load_sem.at[3]),
    ]
    for cp in loads:
        cp.start()
    for cp in loads[:3]:
        cp.wait()
    hot = hot_in[...]
    cold = owner_in[...] * TOUCHED + slot_in[...]
    ids[0, 0:4, :] = hot[0:4] + hot[4:8] * 65536
    ids[0, 4:6, :] = cold[0:2] + cold[2:4] * 65536
    ids[0, 6:8, :] = jnp.zeros((2, SAMP), jnp.int32)
    loads[3].wait()

    pl.semaphore_wait(barrier, (NDP - 1) + (NY - 1) + (NZ - 1))

    pending = []
    for k, e in dp_offsets:
        there = ((NX - k) % NX) * NC + e
        cp = pltpu.make_async_remote_copy(
            src_ref=ids.at[0], dst_ref=ids.at[there], send_sem=id_send.at[there], recv_sem=id_recv.at[there],
            device_id=dp_peer(k, e), device_id_type=LOGICAL)
        cp.start()
        pending.append(cp)
    for k in (2, 1, 3):
        there = (NX - k) * NC
        cp = pltpu.make_async_remote_copy(
            src_ref=cot.at[0], dst_ref=cot.at[there], send_sem=cot_send.at[k], recv_sem=cot_recv.at[there],
            device_id=dp_peer(k, 0), device_id_type=LOGICAL)
        cp.start()
        pending.append(cp)

    def forward(dx):
        cp = pltpu.make_async_remote_copy(
            src_ref=cot.at[dx * NC], dst_ref=cot.at[dx * NC + 1], send_sem=fwd_send.at[dx],
            recv_sem=cot_recv.at[dx * NC + 1], device_id=dp_peer(0, 1), device_id_type=LOGICAL)
        cp.start()
        pending.append(cp)

    forward(0)

    def wait_id(g):
        pltpu.make_async_remote_copy(
            src_ref=ids.at[g], dst_ref=ids.at[g], send_sem=id_send.at[g], recv_sem=id_recv.at[g],
            device_id=dp_peer(0, 1), device_id_type=LOGICAL).wait_recv()

    def wait_cot(g):
        pltpu.make_async_remote_copy(
            src_ref=cot.at[g], dst_ref=cot.at[g], send_sem=cot_send.at[0], recv_sem=cot_recv.at[g],
            device_id=dp_peer(0, 1), device_id_type=LOGICAL).wait_recv()

    row = lax.broadcasted_iota(jnp.int32, (NY * NZ, SAMP), 0)
    order = (row // (NY * PER)) * PER + row % PER
    zrel = jnp.where(order % 2 == 0, NZ // 2 + order // 2, NZ // 2 - 1 - order // 2)
    yrel = (row // PER) % NY
    owner_of = ((y + yrel) % NY) * NZ + (z + zrel) % NZ
    slot_row = lax.broadcasted_iota(jnp.int32, (COLD_SHARE, SAMP), 0) + d * COLD_SHARE

    def hot_codes(q, r):
        i = lax.broadcasted_iota(jnp.int32, (PER * HOT_SHARE, SAMP), 0)
        n = q * PER + i // HOT_SHARE
        rel = jnp.where(n % 2 == 0, NZ // 2 + n // 2, NZ // 2 - 1 - n // 2)
        own = ((y + r) % NY) * NZ + (z + rel) % NZ
        return (own * HOT_SHARE + i % HOT_SHARE).astype(jnp.float32).astype(jnp.bfloat16)

    def build(g):
        block = ids[g]
        lo = block & 65535
        hi = block // 65536
        cold_ids = [lo[4:5], lo[5:6], hi[4:5], hi[5:6]]
        value = jnp.full((NY * NZ, SAMP), -1, jnp.int32)
        for v in cold_ids:
            value = jnp.where(v // TOUCHED == owner_of, v % TOUCHED, value)
        slotfor[...] = value
        hot_ids = []
        for half in (lo, hi):
            sub = half[0:4] & (HOT_LOCAL - 1)
            code = (half[0:4] // HOT_LOCAL) * HOT_SHARE + (sub & (HOT_SHARE - 1))
            code = jnp.where(sub // HOT_SHARE == d, code, -1)
            for j in range(4):
                hot_ids.append(jnp.broadcast_to(code[j:j + 1], (PER * HOT_SHARE, SAMP)).astype(jnp.float32).astype(jnp.bfloat16))
        columns = pl.ds(pl.multiple_of(g * SAMP, SAMP), SAMP)
        for q in range(CHUNKS):
            for r in range(NY):
                for k in range(PER):
                    ell = (q * NY + r) * PER + k
                    match = slotfor[ell:ell + 1, :] == slot_row
                    counts[q, pl.ds(r * BLOCK + k * COLD_SHARE, COLD_SHARE), columns] = jnp.where(match, 1.0, 0.0).astype(jnp.bfloat16)
                codes = hot_codes(q, r)
                total = jnp.zeros((PER * HOT_SHARE, SAMP), jnp.bfloat16)
                for v in hot_ids:
                    total = total + jnp.where(v == codes, jnp.bfloat16(1), jnp.bfloat16(0))
                counts[q, pl.ds(r * BLOCK + PER * COLD_SHARE, PER * HOT_SHARE), columns] = total

    def build_step(g, carry):
        @pl.when(g > 0)
        def _():
            wait_id(g)
        build(g)
        return carry

    lax.fori_loop(0, NDP, build_step, 0)

    for dx in (1, 3, 2):
        wait_cot(dx * NC)
        forward(dx)
    for dx in range(NX):
        wait_cot(dx * NC + 1)

    everything = cot[...].reshape(NDP * SAMP, FEAT)
    for q in range(CHUNKS):
        part = jnp.dot(counts[q], everything, preferred_element_type=jnp.float32)
        psum_own[q] = part[0:BLOCK]
        for r in range(1, NY):
            ysend[q, r - 1] = part[r * BLOCK:(r + 1) * BLOCK].astype(jnp.bfloat16)
            cp = pltpu.make_async_remote_copy(
                src_ref=ysend.at[q, r - 1], dst_ref=yrecv.at[q, NY - 1 - r], send_sem=y_send.at[q, r - 1],
                recv_sem=y_recv.at[q, NY - 1 - r], device_id=y_peer(r), device_id_type=LOGICAL)
            cp.start()
            pending.append(cp)

    for q in range(CHUNKS):
        total = psum_own[q]
        for r in range(NY - 1):
            pltpu.make_async_remote_copy(
                src_ref=yrecv.at[q, r], dst_ref=yrecv.at[q, r], send_sem=y_send.at[q, r], recv_sem=y_recv.at[q, r],
                device_id=y_peer(1), device_id_type=LOGICAL).wait_recv()
            total = total + yrecv[q, r].astype(jnp.float32)
        for k in range(PER):
            n = q * PER + k
            rel = Z_ORDER[n]
            cold_part = total[k * COLD_SHARE:(k + 1) * COLD_SHARE]
            base = PER * COLD_SHARE + k * HOT_SHARE
            hot_part = total[base:base + HOT_SHARE]
            packed = [
                cold_part[:, :128],
                cold_part[:, 128:],
                jnp.concatenate([hot_part[:, :128], hot_part[:, 128:], jnp.zeros((8, 128), jnp.float32)], axis=0),
            ]
            for i in range(3):
                if rel == 0:
                    zown[i] = packed[i]
                else:
                    zsend[n, i] = packed[i].astype(jnp.bfloat16)
            if rel:
                there = Z_ORDER.index(NZ - rel)
                cp = pltpu.make_async_remote_copy(
                    src_ref=zsend.at[n], dst_ref=zrecv.at[there], send_sem=z_send.at[n], recv_sem=z_recv.at[there],
                    device_id=z_peer(rel), device_id_type=LOGICAL)
                cp.start()
                pending.append(cp)

    total = [zown[i] for i in range(3)]
    for n in reversed(range(NZ - 1)):
        pltpu.make_async_remote_copy(
            src_ref=zsend.at[n], dst_ref=zrecv.at[n], send_sem=z_send.at[n], recv_sem=z_recv.at[n],
            device_id=z_peer(1), device_id_type=LOGICAL).wait_recv()
        total = [total[i] + zrecv[n, i].astype(jnp.float32) for i in range(3)]
    fbuf[d, 0:16, :] = total[0]
    fbuf[d, 16:32, :] = total[1]
    fbuf[d, 32:40, :] = total[2][0:8]
    for i, (k, e) in enumerate(dp_offsets):
        cp = pltpu.make_async_remote_copy(
            src_ref=fbuf.at[d], dst_ref=fbuf.at[d], send_sem=f_send.at[i], recv_sem=f_recv.at[d],
            device_id=dp_peer(k, e), device_id_type=LOGICAL)
        cp.start()
        pending.append(cp)
    for k, e in dp_offsets:
        sender = dp_peer(k, e)[0]
        pltpu.make_async_remote_copy(
            src_ref=fbuf.at[sender], dst_ref=fbuf.at[sender], send_sem=f_send.at[0], recv_sem=f_recv.at[sender],
            device_id=dp_peer(k, e), device_id_type=LOGICAL).wait_recv()
    out[...] = fbuf[...]
    for cp in pending:
        cp.wait_send()


def adam(weight, one, two, gradient):
    row_norm = jnp.sqrt(jnp.sum(gradient * gradient, axis=1, keepdims=True))
    clipped = gradient * (CLIP_NORM / jnp.maximum(row_norm, CLIP_NORM))
    first = BETA_ONE * one + (1.0 - BETA_ONE) * clipped
    second = BETA_TWO * two + (1.0 - BETA_TWO) * clipped * clipped
    correct_one = 1.0 - BETA_ONE**STEP
    correct_two = 1.0 - BETA_TWO**STEP
    stepped = weight - LEARN_RATE * (first / correct_one) / (jnp.sqrt(second / correct_two) + ADAM_EPS)
    return stepped, first, second


def adam_kernel(live, grads, hw, h1, h2, cw, c1, c2, ohw, oh1, oh2, ocw, oc1, oc2):
    count = live[0]
    for d in range(NDP):
        rows = slice(d * COLD_SHARE, (d + 1) * COLD_SHARE)
        gradient = jnp.concatenate([grads[d, 0:16, :], grads[d, 16:32, :]], axis=1)
        old = (cw[rows, :], c1[rows, :], c2[rows, :])
        new = adam(*old, gradient)
        active = lax.broadcasted_iota(jnp.int32, (COLD_SHARE, FEAT), 0) + d * COLD_SHARE < count
        for ref, a, b in zip((ocw, oc1, oc2), new, old):
            ref[rows, :] = jnp.where(active, a, b)
    left = jnp.concatenate([grads[d, 32:36, :] for d in range(NDP)], axis=0)
    right = jnp.concatenate([grads[d, 36:40, :] for d in range(NDP)], axis=0)
    new = adam(hw[...], h1[...], h2[...], jnp.concatenate([left, right], axis=1))
    for ref, a in zip((ohw, oh1, oh2), new):
        ref[...] = a
    for start in range(TOUCHED, WINDOW, 32):
        rows = slice(start, start + 32)
        old = (cw[rows, :], c1[rows, :], c2[rows, :])
        new = adam(*old, jnp.zeros((32, FEAT), jnp.float32))
        active = lax.broadcasted_iota(jnp.int32, (32, FEAT), 0) + start < count
        for ref, a, b in zip((ocw, oc1, oc2), new, old):
            ref[rows, :] = jnp.where(active, a, b)


def per_device(cotangent, hot_ids, cold_owner, cold_slot, live_rows, hw, h1, h2, cw, c1, c2):
    vmem = pl.BlockSpec(memory_space=pltpu.VMEM)
    anywhere = pl.BlockSpec(memory_space=pl.ANY)
    dma = pltpu.SemaphoreType.DMA
    bf16, f32, i32 = jnp.bfloat16, jnp.float32, jnp.int32
    grads = pl.pallas_call(
        comm_kernel,
        name="gradients",
        out_shape=jax.ShapeDtypeStruct((NDP, 40, 128), f32),
        in_specs=[anywhere] * 4,
        out_specs=vmem,
        scratch_shapes=[
            pltpu.VMEM((8, SAMP), i32),
            pltpu.VMEM((4, SAMP), i32),
            pltpu.VMEM((4, SAMP), i32),
            pltpu.VMEM((NDP, 8, SAMP), i32),
            pltpu.VMEM((NDP, SAMP, FEAT), bf16),
            pltpu.VMEM((NY * NZ, SAMP), i32),
            pltpu.VMEM((CHUNKS, NY * BLOCK, NDP * SAMP), bf16),
            pltpu.VMEM((CHUNKS, BLOCK, FEAT), f32),
            pltpu.VMEM((CHUNKS, NY - 1, BLOCK, FEAT), bf16),
            pltpu.VMEM((CHUNKS, NY - 1, BLOCK, FEAT), bf16),
            pltpu.VMEM((3, 16, 128), f32),
            pltpu.VMEM((NZ, 3, 16, 128), bf16),
            pltpu.VMEM((NZ, 3, 16, 128), bf16),
            pltpu.VMEM((NDP, 40, 128), f32),
            dma((4,)),
            dma((NDP,)),
            dma((NDP,)),
            dma((NX,)),
            dma((NX,)),
            dma((NDP,)),
            dma((CHUNKS, NY - 1)),
            dma((CHUNKS, NY - 1)),
            dma((NZ,)),
            dma((NZ,)),
            dma((NDP,)),
            dma((NDP,)),
        ],
        compiler_params=pltpu.CompilerParams(collective_id=0, has_side_effects=True, vmem_limit_bytes=32 * 1024 * 1024),
    )(cotangent, hot_ids.T, cold_owner.T, cold_slot.T)
    smem = pl.BlockSpec(memory_space=pltpu.SMEM)
    state = (hw, h1, h2, cw, c1, c2)
    return pl.pallas_call(
        adam_kernel,
        name="adam",
        out_shape=[jax.ShapeDtypeStruct(a.shape, a.dtype) for a in state],
        in_specs=[smem] + [vmem] * 7,
        out_specs=[vmem] * 6,
    )(live_rows, grads, *state)


def solution(mesh):
    rows = P(("dp", "table"), None)
    shard = P("table", None)
    return jax.shard_map(
        per_device, mesh=mesh, in_specs=(rows,) * 4 + (P("table"),) + (shard,) * 6, out_specs=(shard,) * 6,
        check_vma=False)
```

time: 667 us -> 55.6 us (0.08)
  waiting for transfers between devices: 552 us -> 0 us
  Pallas kernels: 0 us -> 51 us
  other arithmetic: 49.7 us -> 0 us
  starting transfers between devices: 26.9 us -> 0 us
  between operations: 16.5 us -> 1.32 us
  local copies, waits for them, and re-layouts: 16 us -> 2.96 us
    psum x2 -> x0, waiting for transfers between devices: 545 us -> none  [the longest x1 476 us: per_device(): summed = lax.psum(pieces.reshape(row_count, features), ('dp', 'table'))]
    pallas_call x0 -> x2, Pallas kernels: none -> 51 us  [the longest x1 48.6 us: per_device(): pl.pallas_call(comm_kernel, name='gradients', out_shape=jax.ShapeDtypeStr...]
    all_to_all x2 -> x0, starting transfers between devices: 26.8 us -> none  [the longest x1 19.3 us: per_device(): lax.all_to_all(out_slots.reshape(shards, capacity), 'table', split_axis=0...]
    reduce_sum x7 -> x0, other arithmetic: 23.8 us -> none  [the longest x4 21.9 us: hot_block(): hits = jnp.sum(matches, axis=2).astype(jnp.bfloat16)]
    another operation x3 -> x0, other arithmetic: 18.2 us -> none
    scatter x2 -> x0, local copies, waits for them, and re-layouts: 10.2 us -> none  [the longest x1 5.87 us: per_device(): jnp.zeros((shards * capacity, features), jnp.bfloat16).at[target]]
    all_to_all x2 -> x0, waiting for transfers between devices: 7.04 us -> none  [the longest x1 7.04 us: per_device(): lax.all_to_all(out_slots.reshape(shards, capacity), 'table', split_axis=0...]
  transfers between devices with their start and end apart: 4 -> 0, of which waited for: 3 -> 0; matrix products, arithmetic and copies ran while one was open for 6% -> 0% of each run, Pallas kernels for 0% -> 0%
where the time goes in v1:
time: 55.6 us; the launch traced here: 55.3 us
  Pallas kernels  51 us (92%)
  local copies, waits for them, and re-layouts  2.96 us (5%)
  between operations  1.32 us (2%)
    pallas_call x1, Pallas kernels, per_device(): pl.pallas_call(comm_kernel, name='gradients', out_shape=jax.ShapeDtypeStr...  48.6 us
    unnamed x10, local copies, waits for them, and re-layouts  2.96 us
    pallas_call x1, Pallas kernels, per_device(): pl.pallas_call(adam_kernel, name='adam', out_shape=[jax.ShapeDtypeStruct(...  2.44 us

profile of v1, /device:TPU:1, one launch (start us, length us, event | category | flops | bytes accessed | tf_op | source)
XLA Modules:
  0.0 55.3 jit_solution(8305790148661902767)
XLA Ops:
  0.6 0.0 copy-start.3
  1.3 0.0 copy-done.3
  1.3 0.0 copy-start.1
  1.3 0.9 %copy-done.1 = bf16[256,256]{1,0:T(8,128)(2,1)S(1)} copy-done((bf16[256,256]{1,0:T(8,128)(2,1)S(1)}, bf16[256,256]{1,0:T(8,128)(2,1)}, u32[]{:S(2)}) %copy-start.1) | copy-done | bytes 131096
  2.2 0.0 copy-start.2
  2.2 0.7 %copy-done.2 = s32[256,8]{0,1:T(8,128)S(1)} copy-done((s32[256,8]{0,1:T(8,128)S(1)}, s32[256,8]{0,1:T(8,128)}, u32[]{:S(2)}) %copy-start.2) | copy-done | bytes 8216
  2.9 0.0 copy-start.4
  2.9 0.7 %copy-done.4 = s32[256,4]{0,1:T(4,128)S(1)} copy-done((s32[256,4]{0,1:T(4,128)S(1)}, s32[256,4]{0,1:T(4,128)}, u32[]{:S(2)}) %copy-start.4) | copy-done | bytes 4120
  3.6 48.6 %gradients.1.grads = f32[8,40,128]{2,1,0:T(8,128)S(1)} custom-call(bf16[256,256]{1,0:T(8,128)(2,1)S(1)} %copy-done.1, s32[8,256]{1,0:T(8,128)S(1)} %bitcast.3, s32[4,256]{1,0:T(4,128)S(1)} %bitcast.4, s32[4,256]{1,0:T(4,128)S(1)} %bitcast.5), custom_call_target="tpu_custom_call" | custom-call | tf_op jit(solution)/shard_map/gradients/pallas_call | solution.py:283
  52.2 0.0 copy-start
  52.2 0.6 %copy-done = f32[8,40,128]{2,1,0:T(8,128)} copy-done((f32[8,40,128]{2,1,0:T(8,128)}, f32[8,40,128]{2,1,0:T(8,128)S(1)}, u32[]{:S(2)}) %copy-start) | copy-done | bytes 163864
  52.9 2.4 %adam.1 = (f32[32,256]{1,0:T(8,128)}, f32[32,256]{1,0:T(8,128)}, f32[32,256]{1,0:T(8,128)}, f32[256,256]{1,0:T(8,128)}, f32[256,256]{1,0:T(8,128)}, /*index=5*/f32[256,256]{1,0:T(8,128)}) custom-call(s32[1]{0:T(128)S(6)} %copy.17.live, f32[8,40,128]{2,1,0:T(8,128)} %copy-done, f32[32,256]{1,0:T(8,128)} %hw.1, f32[32,256]{1,0:T(8,128)} %h1.1, f32[32,256]{1,0:T(8,128)} %h2.1, ...), custom_call_target="tpu_custom_call" | custom-call | tf_op jit(solution)/shard_map/adam/pallas_call | solution.py:321
Async XLA Ops:
  0.6 0.7 %copy-start.3 = (s32[256,4]{0,1:T(4,128)S(1)}, s32[256,4]{0,1:T(4,128)}, u32[]{:S(2)}) copy-start(s32[256,4]{0,1:T(4,128)} %param.13) | copy-start | bytes 12292
  1.3 0.9 %copy-start.1 = (bf16[256,256]{1,0:T(8,128)(2,1)S(1)}, bf16[256,256]{1,0:T(8,128)(2,1)}, u32[]{:S(2)}) copy-start(bf16[256,256]{1,0:T(8,128)(2,1)} %cot_hbm.1) | copy-start | bytes 393220
  2.2 0.7 %copy-start.2 = (s32[256,8]{0,1:T(8,128)S(1)}, s32[256,8]{0,1:T(8,128)}, u32[]{:S(2)}) copy-start(s32[256,8]{0,1:T(8,128)} %param.12) | copy-start | bytes 24580
  2.9 0.7 %copy-start.4 = (s32[256,4]{0,1:T(4,128)S(1)}, s32[256,4]{0,1:T(4,128)}, u32[]{:S(2)}) copy-start(s32[256,4]{0,1:T(4,128)} %param.14) | copy-start | bytes 12292
  52.2 0.7 %copy-start = (f32[8,40,128]{2,1,0:T(8,128)}, f32[8,40,128]{2,1,0:T(8,128)S(1)}, u32[]{:S(2)}) copy-start(f32[8,40,128]{2,1,0:T(8,128)S(1)} %gradients.1.grads) | copy-start | bytes 491524

commit v2 on v1

--- a/solution.py
+++ b/solution.py
@@ -33,7 +33,7 @@
 def comm_kernel(
     cot_hbm, hot_hbm, owner_hbm, slot_hbm, out,
     hot_in, owner_in, slot_in, ids, cot, slotfor, counts, psum_own, ysend, yrecv, zown, zsend, zrecv, fbuf,
-    load_sem, id_send, id_recv, cot_send, fwd_send, cot_recv, y_send, y_recv, z_send, z_recv, f_send, f_recv,
+    load_sem, id_send, id_recv, cot_send, fwd_send, cot_recv, y_send, y_recv, z_send, z_recv, f_send, f_recv, tokens,
 ):
     d = lax.axis_index("dp")
     t = lax.axis_index("table")
@@ -53,12 +53,7 @@
     dp_offsets = [(k, e) for k in range(NX) for e in range(NC) if (k, e) != (0, 0)]
 
     barrier = pltpu.get_barrier_semaphore()
-    for r in sorted(range(1, NZ), key=lambda r: -min(r, NZ - r)):
-        pl.semaphore_signal(barrier, inc=1, device_id=z_peer(r), device_id_type=LOGICAL)
-    for r in range(1, NY):
-        pl.semaphore_signal(barrier, inc=1, device_id=y_peer(r), device_id_type=LOGICAL)
-    for k, e in dp_offsets:
-        pl.semaphore_signal(barrier, inc=1, device_id=dp_peer(k, e), device_id_type=LOGICAL)
+    near_z = (1, 2, NZ - 2, NZ - 1)
 
     loads = [
         pltpu.make_async_copy(hot_hbm, hot_in, load_sem.at[0]),
@@ -68,6 +63,12 @@
     ]
     for cp in loads:
         cp.start()
+    for k, e in dp_offsets:
+        pl.semaphore_signal(barrier, inc=1, device_id=dp_peer(k, e), device_id_type=LOGICAL)
+    for r in range(1, NY):
+        pl.semaphore_signal(barrier, inc=1, device_id=y_peer(r), device_id_type=LOGICAL)
+    for r in near_z:
+        pl.semaphore_signal(barrier, inc=1, device_id=z_peer(r), device_id_type=LOGICAL)
     for cp in loads[:3]:
         cp.wait()
     hot = hot_in[...]
@@ -75,9 +76,7 @@
     ids[0, 0:4, :] = hot[0:4] + hot[4:8] * 65536
     ids[0, 4:6, :] = cold[0:2] + cold[2:4] * 65536
     ids[0, 6:8, :] = jnp.zeros((2, SAMP), jnp.int32)
-    loads[3].wait()
-
-    pl.semaphore_wait(barrier, (NDP - 1) + (NY - 1) + (NZ - 1))
+    pl.semaphore_wait(barrier, (NDP - 1) + (NY - 1) + len(near_z))
 
     pending = []
     for k, e in dp_offsets:
@@ -90,7 +89,7 @@
     for k in (2, 1, 3):
         there = (NX - k) * NC
         cp = pltpu.make_async_remote_copy(
-            src_ref=cot.at[0], dst_ref=cot.at[there], send_sem=cot_send.at[k], recv_sem=cot_recv.at[there],
+            src_ref=cot_hbm, dst_ref=cot.at[there], send_sem=cot_send.at[k], recv_sem=cot_recv.at[there],
             device_id=dp_peer(k, 0), device_id_type=LOGICAL)
         cp.start()
         pending.append(cp)
@@ -102,7 +101,10 @@
         cp.start()
         pending.append(cp)
 
+    loads[3].wait()
     forward(0)
+    for r, i in ((2, 1), (NZ - 2, 0)):
+        pl.semaphore_signal(tokens.at[i], inc=1, device_id=z_peer(r), device_id_type=LOGICAL)
 
     def wait_id(g):
         pltpu.make_async_remote_copy(
@@ -169,6 +171,10 @@
     for dx in (1, 3, 2):
         wait_cot(dx * NC)
         forward(dx)
+    pl.semaphore_wait(tokens.at[0], 1)
+    pl.semaphore_wait(tokens.at[1], 1)
+    for r, i in ((4, 3), (NZ - 4, 2)):
+        pl.semaphore_signal(tokens.at[i], inc=1, device_id=z_peer(r), device_id_type=LOGICAL)
     for dx in range(NX):
         wait_cot(dx * NC + 1)
 
@@ -184,6 +190,8 @@
             cp.start()
             pending.append(cp)
 
+    pl.semaphore_wait(tokens.at[2], 1)
+    pl.semaphore_wait(tokens.at[3], 1)
     for q in range(CHUNKS):
         total = psum_own[q]
         for r in range(NY - 1):
@@ -221,9 +229,8 @@
             src_ref=zsend.at[n], dst_ref=zrecv.at[n], send_sem=z_send.at[n], recv_sem=z_recv.at[n],
             device_id=z_peer(1), device_id_type=LOGICAL).wait_recv()
         total = [total[i] + zrecv[n, i].astype(jnp.float32) for i in range(3)]
-    fbuf[d, 0:16, :] = total[0]
-    fbuf[d, 16:32, :] = total[1]
-    fbuf[d, 32:40, :] = total[2][0:8]
+    for i in range(3):
+        fbuf[d, i] = total[i].astype(jnp.bfloat16)
     for i, (k, e) in enumerate(dp_offsets):
         cp = pltpu.make_async_remote_copy(
             src_ref=fbuf.at[d], dst_ref=fbuf.at[d], send_sem=f_send.at[i], recv_sem=f_recv.at[d],
@@ -251,40 +258,74 @@
     return stepped, first, second
 
 
-def adam_kernel(live, grads, hw, h1, h2, cw, c1, c2, ohw, oh1, oh2, ocw, oc1, oc2):
+def adam_kernel(live, grads, *refs):
+    olds, news, held, made, load_sem, store_sem = refs[0:6], refs[6:12], refs[12:18], refs[18:24], refs[24], refs[25]
+    whole = slice(None)
+    parts = [(3, slice(TOUCHED, WINDOW)), (0, whole), (3, slice(0, TOUCHED))]
+    loads = [
+        [pltpu.make_async_copy(olds[a + i].at[rows], held[a + i].at[rows], load_sem.at[p, i]) for i in range(3)]
+        for p, (a, rows) in enumerate(parts)
+    ]
+    stores = [
+        [pltpu.make_async_copy(made[a + i].at[rows], news[a + i].at[rows], store_sem.at[p, i]) for i in range(3)]
+        for p, (a, rows) in enumerate(parts)
+    ]
+    for part in loads:
+        for cp in part:
+            cp.start()
     count = live[0]
+
+    def cold(rows, start, gradient):
+        old = [held[3 + i][rows, :] for i in range(3)]
+        new = adam(*old, gradient)
+        active = lax.broadcasted_iota(jnp.int32, gradient.shape, 0) + start < count
+        for i in range(3):
+            made[3 + i][rows, :] = jnp.where(active, new[i], old[i])
+
+    for cp in loads[0]:
+        cp.wait()
+    for start in range(TOUCHED, WINDOW, 32):
+        cold(slice(start, start + 32), start, jnp.zeros((32, FEAT), jnp.float32))
+    for cp in stores[0]:
+        cp.start()
+
+    for cp in loads[1]:
+        cp.wait()
+    tiles = [grads[d, 2].astype(jnp.float32) for d in range(NDP)]
+    left = jnp.concatenate([tile[0:HOT_SHARE] for tile in tiles], axis=0)
+    right = jnp.concatenate([tile[HOT_SHARE:2 * HOT_SHARE] for tile in tiles], axis=0)
+    new = adam(held[0][...], held[1][...], held[2][...], jnp.concatenate([left, right], axis=1))
+    for i in range(3):
+        made[i][...] = new[i]
+    for cp in stores[1]:
+        cp.start()
+
+    for cp in loads[2]:
+        cp.wait()
     for d in range(NDP):
-        rows = slice(d * COLD_SHARE, (d + 1) * COLD_SHARE)
-        gradient = jnp.concatenate([grads[d, 0:16, :], grads[d, 16:32, :]], axis=1)
-        old = (cw[rows, :], c1[rows, :], c2[rows, :])
-        new = adam(*old, gradient)
-        active = lax.broadcasted_iota(jnp.int32, (COLD_SHARE, FEAT), 0) + d * COLD_SHARE < count
-        for ref, a, b in zip((ocw, oc1, oc2), new, old):
-            ref[rows, :] = jnp.where(active, a, b)
-    left = jnp.concatenate([grads[d, 32:36, :] for d in range(NDP)], axis=0)
-    right = jnp.concatenate([grads[d, 36:40, :] for d in range(NDP)], axis=0)
-    new = adam(hw[...], h1[...], h2[...], jnp.concatenate([left, right], axis=1))
-    for ref, a in zip((ohw, oh1, oh2), new):
-        ref[...] = a
-    for start in range(TOUCHED, WINDOW, 32):
-        rows = slice(start, start + 32)
-        old = (cw[rows, :], c1[rows, :], c2[rows, :])
-        new = adam(*old, jnp.zeros((32, FEAT), jnp.float32))
-        active = lax.broadcasted_iota(jnp.int32, (32, FEAT), 0) + start < count
-        for ref, a, b in zip((ocw, oc1, oc2), new, old):
-            ref[rows, :] = jnp.where(active, a, b)
+        gradient = jnp.concatenate([grads[d, 0], grads[d, 1]], axis=1).astype(jnp.float32)
+        cold(slice(d * COLD_SHARE, (d + 1) * COLD_SHARE), d * COLD_SHARE, gradient)
+    for cp in stores[2]:
+        cp.start()
+    for part in stores:
+        for cp in part:
+            cp.wait()
+
+
+def in_hbm(array):
+    return pltpu.with_memory_space_constraint(array, pltpu.HBM)
 
 
 def per_device(cotangent, hot_ids, cold_owner, cold_slot, live_rows, hw, h1, h2, cw, c1, c2):
     vmem = pl.BlockSpec(memory_space=pltpu.VMEM)
-    anywhere = pl.BlockSpec(memory_space=pl.ANY)
+    hbm = pl.BlockSpec(memory_space=pltpu.HBM)
     dma = pltpu.SemaphoreType.DMA
     bf16, f32, i32 = jnp.bfloat16, jnp.float32, jnp.int32
     grads = pl.pallas_call(
         comm_kernel,
         name="gradients",
-        out_shape=jax.ShapeDtypeStruct((NDP, 40, 128), f32),
-        in_specs=[anywhere] * 4,
+        out_shape=jax.ShapeDtypeStruct((NDP, 3, 16, 128), bf16),
+        in_specs=[hbm] * 4,
         out_specs=vmem,
         scratch_shapes=[
             pltpu.VMEM((8, SAMP), i32),
@@ -300,7 +341,7 @@
             pltpu.VMEM((3, 16, 128), f32),
             pltpu.VMEM((NZ, 3, 16, 128), bf16),
             pltpu.VMEM((NZ, 3, 16, 128), bf16),
-            pltpu.VMEM((NDP, 40, 128), f32),
+            pltpu.VMEM((NDP, 3, 16, 128), bf16),
             dma((4,)),
             dma((NDP,)),
             dma((NDP,)),
@@ -313,18 +354,20 @@
             dma((NZ,)),
             dma((NDP,)),
             dma((NDP,)),
+            pltpu.SemaphoreType.REGULAR((4,)),
         ],
         compiler_params=pltpu.CompilerParams(collective_id=0, has_side_effects=True, vmem_limit_bytes=32 * 1024 * 1024),
-    )(cotangent, hot_ids.T, cold_owner.T, cold_slot.T)
+    )(in_hbm(cotangent), in_hbm(hot_ids.T), in_hbm(cold_owner.T), in_hbm(cold_slot.T))
     smem = pl.BlockSpec(memory_space=pltpu.SMEM)
     state = (hw, h1, h2, cw, c1, c2)
     return pl.pallas_call(
         adam_kernel,
         name="adam",
         out_shape=[jax.ShapeDtypeStruct(a.shape, a.dtype) for a in state],
-        in_specs=[smem] + [vmem] * 7,
-        out_specs=[vmem] * 6,
-    )(live_rows, grads, *state)
+        in_specs=[smem, vmem] + [hbm] * 6,
+        out_specs=[hbm] * 6,
+        scratch_shapes=[pltpu.VMEM(a.shape, a.dtype) for a in state * 2] + [dma((3, 3)), dma((3, 3))],
+    )(live_rows, pltpu.with_memory_space_constraint(grads, pltpu.VMEM), *(in_hbm(a) for a in state))
 
 
 def solution(mesh):

time: 55.6 us -> 49.8 us (0.90)
  local copies, waits for them, and re-layouts: 2.96 us -> 0 us
  Pallas kernels: 51 us -> 48.3 us
    unnamed x10 -> x0, local copies, waits for them, and re-layouts: 2.96 us -> none
    pallas_call x1, Pallas kernels: 48.6 us -> 45.8 us  [per_device(): pl.pallas_call(comm_kernel, name='gradients', out_shape=jax.ShapeDtypeStr...]
where the time goes in v2:
time: 49.8 us; the launch traced here: 49.6 us
  Pallas kernels  48.3 us (97%)
  between operations  1.29 us (3%)
    pallas_call x1, Pallas kernels, per_device(): pl.pallas_call(comm_kernel, name='gradients', out_shape=jax.ShapeDtypeStr...  45.8 us
    pallas_call x1, Pallas kernels, per_device(): pl.pallas_call(adam_kernel, name='adam', out_shape=[jax.ShapeDtypeStruct(...  2.5 us

profile of v2, /device:TPU:1, one launch (start us, length us, event | category | flops | bytes accessed | tf_op | source)
XLA Modules:
  0.0 49.6 jit_solution(16296209970016360632)
XLA Ops:
  1.3 45.8 %gradients.1.grads = bf16[8,3,16,128]{3,2,1,0:T(8,128)(2,1)S(1)} custom-call(bf16[256,256]{1,0:T(8,128)(2,1)} %cot_hbm.1, s32[8,256]{1,0:T(8,128)} %bitcast.3, s32[4,256]{1,0:T(4,128)} %bitcast.4, s32[4,256]{1,0:T(4,128)} %bitcast.5), custom_call_target="tpu_custom_call" | custom-call | tf_op jit(solution)/shard_map/gradients/pallas_call | solution.py:324
  47.1 2.5 %adam.1 = (f32[32,256]{1,0:T(8,128)}, f32[32,256]{1,0:T(8,128)}, f32[32,256]{1,0:T(8,128)}, f32[256,256]{1,0:T(8,128)}, f32[256,256]{1,0:T(8,128)}, /*index=5*/f32[256,256]{1,0:T(8,128)}) custom-call(s32[1]{0:T(128)S(6)} %copy.17.live, bf16[8,3,16,128]{3,2,1,0:T(8,128)(2,1)S(1)} %gradients.1.grads, f32[32,256]{1,0:T(8,128)} %refs_0_.1, f32[32,256]{1,0:T(8,128)} %refs_1_.1, ...), custom_call_target="tpu_custom_call" | custom-call | tf_op jit(solution)/shard_map/adam/pallas_call | solution.py:363

commit v3 on v2

v3 whole, which is shorter than its diff:
```python
import functools

import jax
import jax.numpy as jnp
from jax import lax
from jax.experimental import pallas as pl
from jax.experimental.pallas import tpu as pltpu
from jax.sharding import PartitionSpec as P

STEP = 3
BETA_ONE = 0.9
BETA_TWO = 0.999
ADAM_EPS = 1e-08
LEARN_RATE = 0.05
CLIP_NORM = 4.0

NX, NC, NY, NZ = 4, 2, 4, 16
SAMP = 256
FEAT = 256
HALF = FEAT // 2
HOT_LOCAL = 32
WINDOW = 256
TOUCHED = 128
NDP = NX * NC
HOT_SHARE = HOT_LOCAL // NDP
COLD_SHARE = TOUCHED // NDP
CHUNKS = 4
PER = NZ // CHUNKS
BLOCK = PER * (COLD_SHARE + HOT_SHARE)
Z_ORDER = [NZ // 2 + n // 2 if n % 2 == 0 else NZ // 2 - 1 - n // 2 for n in range(NZ)]
FOLD = 4
FAR = [r for r in Z_ORDER if FOLD < r < NZ - FOLD]
KEPT = [0, FOLD, NZ - FOLD]
LOGICAL = pl.DeviceIdType.MESH


def comm_kernel(
    cot_hbm, hot_hbm, owner_hbm, slot_hbm, s0, s1, s2, s3, s4, s5, out, o0, o1, o2, o3, o4, o5,
    hot_in, owner_in, slot_in, ids, cot, owner_rows, code_rows, slotfor, counts, part, psum_own, rsend, rrecv, zown,
    zsend, zrecv, zfar, fbuf,
    load_sem, state_sem, id_send, id_recv, cot_send, fwd_send, cot_recv, r_send, r_recv, z_send, z_recv, far_recv, f_send, f_recv,
    tokens,
):
    d = lax.axis_index("dp")
    t = lax.axis_index("table")
    x, c = d // NC, d % NC
    y, z = t // NZ, t % NZ

    def peer(axis, k, e=0):
        core = (1 - c) if e else c
        if axis == 0:
            return (lax.rem(x + k, NX) * NC + core, t)
        return (x * NC + core, lax.rem(y + k, NY) * NZ + z)

    def z_peer(r):
        return (d, y * NZ + lax.rem(z + r, NZ))

    partner = peer(0, 0, 1)
    offsets = [(k, e) for k in (2, 1, 3) for e in range(NC)]
    dp_peers = [partner] + [peer(0, k, e) for k, e in offsets]
    pending = []

    def send(src, dst, send_sem, recv_sem, device):
        cp = pltpu.make_async_remote_copy(
            src_ref=src, dst_ref=dst, send_sem=send_sem, recv_sem=recv_sem, device_id=device, device_id_type=LOGICAL)
        cp.start()
        pending.append(cp)

    def arrive(ref, recv_sem):
        pltpu.make_async_remote_copy(
            src_ref=ref, dst_ref=ref, send_sem=f_send.at[0], recv_sem=recv_sem, device_id=partner,
            device_id_type=LOGICAL).wait_recv()

    def signal(semaphore, device):
        pl.semaphore_signal(semaphore, inc=1, device_id=device, device_id_type=LOGICAL)

    loads = [
        pltpu.make_async_copy(hot_hbm, hot_in, load_sem.at[0]),
        pltpu.make_async_copy(owner_hbm, owner_in, load_sem.at[1]),
        pltpu.make_async_copy(slot_hbm, slot_in, load_sem.at[2]),
    ] + [
        pltpu.make_async_copy(cot_hbm.at[:, pl.ds(h * HALF, HALF)], cot.at[h, 0], load_sem.at[3 + h]) for h in range(2)
    ]
    for cp in loads:
        cp.start()
    barrier = pltpu.get_barrier_semaphore()
    near = [partner] + [peer(h, k) for h in range(2) for k in (2, 1, 3)] + [z_peer(r) for r in (1, 2, NZ - 2, NZ - 1)]
    for device in near:
        signal(barrier, device)
    states = [
        pltpu.make_async_copy(a, b, state_sem.at[i])
        for i, (a, b) in enumerate(zip((s0, s1, s2, s3, s4, s5), (o0, o1, o2, o3, o4, o5)))
    ]
    for cp in states:
        cp.start()

    row = lax.broadcasted_iota(jnp.int32, (NY * NZ, SAMP), 0)
    order = (row // (NY * PER)) * PER + row % PER
    zrel = jnp.where(order % 2 == 0, NZ // 2 + order // 2, NZ // 2 - 1 - order // 2)
    yrel = (row // PER) % NY
    owner_rows[0] = ((y + yrel) % NY) * NZ + (z + zrel) % NZ
    owner_rows[1] = y * NZ + (z + zrel) % NZ
    i = lax.broadcasted_iota(jnp.int32, (PER * HOT_SHARE, SAMP), 0)
    for q in range(CHUNKS):
        n = q * PER + i // HOT_SHARE
        rel = jnp.where(n % 2 == 0, NZ // 2 + n // 2, NZ // 2 - 1 - n // 2)
        zz = (z + rel) % NZ
        for r in range(NY):
            first = (((y + r) % NY) * NZ + zz) * HOT_SHARE + i % HOT_SHARE
            second = (zz * NX + (x + r) % NX) * HOT_SHARE + i % HOT_SHARE
            code_rows[0, q, r] = first.astype(jnp.float32).astype(jnp.bfloat16)
            code_rows[1, q, r] = second.astype(jnp.float32).astype(jnp.bfloat16)
    lanes = lax.broadcasted_iota(jnp.int32, (COLD_SHARE, SAMP), 0)

    def build(h, source, g):
        block = ids[source, g]
        lo = block & 65535
        hi = block // 65536
        value = jnp.full((NY * NZ, SAMP), -1, jnp.int32)
        owners = owner_rows[h]
        for v in (lo[4:5], lo[5:6], hi[4:5], hi[5:6]):
            value = jnp.where(v // TOUCHED == owners, v % TOUCHED, value)
        slotfor[...] = value
        hot_ids = []
        for words in (lo, hi):
            shard = words[0:4] // HOT_LOCAL
            share = (words[0:4] % HOT_LOCAL) // HOT_SHARE
            inner = words[0:4] % HOT_SHARE
            if h == 0:
                code = jnp.where(share == d, shard * HOT_SHARE + inner, -1)
            else:
                code = ((shard % NZ) * NX + share // NC) * HOT_SHARE + inner
                code = jnp.where((shard // NZ == y) & (share % NC == c), code, -1)
            for j in range(4):
                wide = jnp.broadcast_to(code[j:j + 1], (PER * HOT_SHARE, SAMP))
                hot_ids.append(wide.astype(jnp.float32).astype(jnp.bfloat16))
        columns = pl.ds(pl.multiple_of(g * SAMP, SAMP), SAMP)
        for q in range(CHUNKS):
            for r in range(NY):
                share = d if h == 0 else lax.rem(x + r, NX) * NC + c
                slots = lanes + share * COLD_SHARE
                for k in range(PER):
                    ell = (q * NY + r) * PER + k
                    match = slotfor[ell:ell + 1, :] == slots
                    counts[h, q, pl.ds(r * BLOCK + k * COLD_SHARE, COLD_SHARE), columns] = jnp.where(match, 1.0, 0.0).astype(jnp.bfloat16)
                codes = code_rows[h, q, r]
                total = jnp.zeros((PER * HOT_SHARE, SAMP), jnp.bfloat16)
                for v in hot_ids:
                    total = total + jnp.where(v == codes, jnp.bfloat16(1), jnp.bfloat16(0))
                counts[h, q, pl.ds(r * BLOCK + PER * COLD_SHARE, PER * HOT_SHARE), columns] = total

    for cp in loads[:3]:
        cp.wait()
    hot = hot_in[...]
    cold = owner_in[...] * TOUCHED + slot_in[...]
    ids[0, 0, 0:4, :] = hot[0:4] + hot[4:8] * 65536
    ids[0, 0, 4:6, :] = cold[0:2] + cold[2:4] * 65536
    ids[0, 0, 6:8, :] = jnp.zeros((2, SAMP), jnp.int32)
    for cp in loads[3:]:
        cp.wait()
    for h in range(2):
        build(h, 0, 0)

    pl.semaphore_wait(barrier, len(near))

    send(ids.at[0, 0], ids.at[0, NX], id_send.at[0, NX], id_recv.at[0, NX], partner)
    for k in (2, 1, 3):
        for h in range(2):
            send(ids.at[0, 0], ids.at[h, NX - k], id_send.at[h, NX - k], id_recv.at[h, NX - k], peer(h, k))

    def forward(h, k):
        send(cot.at[h, k], cot.at[h, NX + k], fwd_send.at[h, k], cot_recv.at[h, NX + k], partner)

    for k in (2, 1, 3):
        for h in range(2):
            send(cot.at[h, 0], cot.at[h, NX - k], cot_send.at[h, k], cot_recv.at[h, NX - k], peer(h, k))
    for h in range(2):
        forward(h, 0)
    for r, i in ((2, 1), (NZ - 2, 0)):
        signal(tokens.at[i], z_peer(r))

    arrive(ids.at[0, NX], id_recv.at[0, NX])
    for h in range(2):
        build(h, 0, NX)
    for k in (1, 3, 2):
        for h in range(2):
            arrive(ids.at[h, k], id_recv.at[h, k])
            send(ids.at[h, k], ids.at[h, NX + k], id_send.at[h, NX + k], id_recv.at[h, NX + k], partner)

    for h in range(2):
        def build_mine(k, carry):
            build(h, h, k)
            return carry

        lax.fori_loop(1, NX, build_mine, 0)
    for h in range(2):
        def build_other(k, carry):
            arrive(ids.at[h, NX + k], id_recv.at[h, NX + k])
            build(h, h, NX + k)
            return carry

        lax.fori_loop(1, NX, build_other, 0)

    for k in (1, 3, 2):
        for h in range(2):
            arrive(cot.at[h, k], cot_recv.at[h, k])
            forward(h, k)

    middle = NX * SAMP
    for h in range(2):
        mine = cot[h, 0:NX].reshape(middle, HALF)
        for q in range(CHUNKS):
            part[h, q] = jnp.dot(counts[h, q, :, 0:middle], mine, preferred_element_type=jnp.float32)
    for h in range(2):
        for k in (0, 1, 3, 2):
            arrive(cot.at[h, NX + k], cot_recv.at[h, NX + k])
    for q in range(CHUNKS):
        for h in range(2):
            others = cot[h, NX:NDP].reshape(middle, HALF)
            done = part[h, q] + jnp.dot(counts[h, q, :, middle:2 * middle], others, preferred_element_type=jnp.float32)
            psum_own[h, q] = done[0:BLOCK]
            for r in (2, 1, 3):
                rsend[h, q, r - 1] = done[r * BLOCK:(r + 1) * BLOCK].astype(jnp.bfloat16)
                there = NY - 1 - r
                send(rsend.at[h, q, r - 1], rrecv.at[h, q, there], r_send.at[h, q, r - 1], r_recv.at[h, q, there], peer(1 - h, r))

    pl.semaphore_wait(tokens.at[0], 1)
    pl.semaphore_wait(tokens.at[1], 1)
    for q in range(CHUNKS):
        totals = []
        for h in range(2):
            total = psum_own[h, q]
            for r in (0, 2, 1):
                arrive(rrecv.at[h, q, r], r_recv.at[h, q, r])
                total = total + rrecv[h, q, r].astype(jnp.float32)
            totals.append(total)
        for k in range(PER):
            n = q * PER + k
            rel = Z_ORDER[n]
            cold_rows = slice(k * COLD_SHARE, (k + 1) * COLD_SHARE)
            base = PER * COLD_SHARE + k * HOT_SHARE
            hot_parts = [total[base:base + HOT_SHARE] for total in totals]
            packed = [total[cold_rows] for total in totals] + [
                jnp.concatenate(hot_parts + [jnp.zeros((8, HALF), jnp.float32)], axis=0)]
            if rel in KEPT:
                for i in range(3):
                    zown[KEPT.index(rel), i] = packed[i]
                continue
            for i in range(3):
                zsend[n, i] = packed[i].astype(jnp.bfloat16)
            if rel in FAR:
                send(zsend.at[n], zfar.at[FAR.index(rel)], z_send.at[n], far_recv.at[FAR.index(rel)],
                     z_peer(rel - FOLD if rel <= NZ // 2 else rel + FOLD))
            else:
                there = Z_ORDER.index(NZ - rel)
                send(zsend.at[n], zrecv.at[there], z_send.at[n], z_recv.at[there], z_peer(rel))

    for rel in (FOLD, NZ - FOLD):
        total = [zown[KEPT.index(rel), i] for i in range(3)]
        for far in FAR:
            if (far <= NZ // 2) == (rel == FOLD):
                arrive(zfar.at[FAR.index(far)], far_recv.at[FAR.index(far)])
                total = [total[i] + zfar[FAR.index(far), i].astype(jnp.float32) for i in range(3)]
        n, there = Z_ORDER.index(rel), Z_ORDER.index(NZ - rel)
        for i in range(3):
            zsend[n, i] = total[i].astype(jnp.bfloat16)
        send(zsend.at[n], zrecv.at[there], z_send.at[n], z_recv.at[there], z_peer(rel))
    while pending:
        pending.pop(0).wait_send()

    total = [zown[0, i] for i in range(3)]
    for rel in (1, NZ - 1, 2, NZ - 2, 3, NZ - 3, FOLD, NZ - FOLD):
        n = Z_ORDER.index(rel)
        arrive(zrecv.at[n], z_recv.at[n])
        total = [total[i] + zrecv[n, i].astype(jnp.float32) for i in range(3)]
    for i in range(3):
        fbuf[d, i] = total[i].astype(jnp.bfloat16)
    for i, device in enumerate(dp_peers):
        send(fbuf.at[d], fbuf.at[d], f_send.at[i], f_recv.at[d], device)
    for cp in states:
        cp.wait()
    for device in dp_peers:
        arrive(fbuf.at[device[0]], f_recv.at[device[0]])
    out[...] = fbuf[...]
    for cp in pending:
        cp.wait_send()


def adam(weight, one, two, gradient):
    row_norm = jnp.sqrt(jnp.sum(gradient * gradient, axis=1, keepdims=True))
    clipped = gradient * (CLIP_NORM / jnp.maximum(row_norm, CLIP_NORM))
    first = BETA_ONE * one + (1.0 - BETA_ONE) * clipped
    second = BETA_TWO * two + (1.0 - BETA_TWO) * clipped * clipped
    correct_one = 1.0 - BETA_ONE**STEP
    correct_two = 1.0 - BETA_TWO**STEP
    stepped = weight - LEARN_RATE * (first / correct_one) / (jnp.sqrt(second / correct_two) + ADAM_EPS)
    return stepped, first, second


def adam_kernel(live, grads, *refs):
    held, news, made, store_sem = refs[0:6], refs[6:12], refs[12:18], refs[18]
    whole = slice(None)
    parts = [(3, slice(TOUCHED, WINDOW)), (0, whole), (3, slice(0, TOUCHED))]
    stores = [
        [pltpu.make_async_copy(made[a + i].at[rows], news[a + i].at[rows], store_sem.at[p, i]) for i in range(3)]
        for p, (a, rows) in enumerate(parts)
    ]
    count = live[0]

    def cold(rows, start, gradient):
        old = [held[3 + i][rows, :] for i in range(3)]
        new = adam(*old, gradient)
        active = lax.broadcasted_iota(jnp.int32, gradient.shape, 0) + start < count
        for i in range(3):
            made[3 + i][rows, :] = jnp.where(active, new[i], old[i])

    for start in range(TOUCHED, WINDOW, 32):
        cold(slice(start, start + 32), start, jnp.zeros((32, FEAT), jnp.float32))
    for cp in stores[0]:
        cp.start()

    tiles = [grads[d, 2].astype(jnp.float32) for d in range(NDP)]
    left = jnp.concatenate([tile[0:HOT_SHARE] for tile in tiles], axis=0)
    right = jnp.concatenate([tile[HOT_SHARE:2 * HOT_SHARE] for tile in tiles], axis=0)
    new = adam(held[0][...], held[1][...], held[2][...], jnp.concatenate([left, right], axis=1))
    for i in range(3):
        made[i][...] = new[i]
    for cp in stores[1]:
        cp.start()

    for d in range(NDP):
        gradient = jnp.concatenate([grads[d, 0], grads[d, 1]], axis=1).astype(jnp.float32)
        cold(slice(d * COLD_SHARE, (d + 1) * COLD_SHARE), d * COLD_SHARE, gradient)
    for cp in stores[2]:
        cp.start()
    for part in stores:
        for cp in part:
            cp.wait()


def per_device(cotangent, hot_ids, cold_owner, cold_slot, live_rows, hw, h1, h2, cw, c1, c2):
    vmem = pl.BlockSpec(memory_space=pltpu.VMEM)
    hbm = pl.BlockSpec(memory_space=pltpu.HBM)
    smem = pl.BlockSpec(memory_space=pltpu.SMEM)
    dma = pltpu.SemaphoreType.DMA
    bf16, f32, i32 = jnp.bfloat16, jnp.float32, jnp.int32
    state = (hw, h1, h2, cw, c1, c2)
    shapes = [jax.ShapeDtypeStruct(a.shape, a.dtype) for a in state]
    operands = (cotangent, hot_ids.T, cold_owner.T, cold_slot.T) + state
    staged = pl.pallas_call(
        comm_kernel,
        name="gradients",
        out_shape=[jax.ShapeDtypeStruct((NDP, 3, COLD_SHARE, HALF), bf16)] + shapes,
        in_specs=[hbm] * len(operands),
        out_specs=[vmem] * 7,
        scratch_shapes=[
            pltpu.VMEM((8, SAMP), i32),
            pltpu.VMEM((4, SAMP), i32),
            pltpu.VMEM((4, SAMP), i32),
            pltpu.VMEM((2, NDP, 8, SAMP), i32),
            pltpu.VMEM((2, NDP, SAMP, HALF), bf16),
            pltpu.VMEM((2, NY * NZ, SAMP), i32),
            pltpu.VMEM((2, CHUNKS, NY, PER * HOT_SHARE, SAMP), bf16),
            pltpu.VMEM((NY * NZ, SAMP), i32),
            pltpu.VMEM((2, CHUNKS, NY * BLOCK, NDP * SAMP), bf16),
            pltpu.VMEM((2, CHUNKS, NY * BLOCK, HALF), f32),
            pltpu.VMEM((2, CHUNKS, BLOCK, HALF), f32),
            pltpu.VMEM((2, CHUNKS, NY - 1, BLOCK, HALF), bf16),
            pltpu.VMEM((2, CHUNKS, NY - 1, BLOCK, HALF), bf16),
            pltpu.VMEM((len(KEPT), 3, COLD_SHARE, HALF), f32),
            pltpu.VMEM((NZ, 3, COLD_SHARE, HALF), bf16),
            pltpu.VMEM((NZ, 3, COLD_SHARE, HALF), bf16),
            pltpu.VMEM((len(FAR), 3, COLD_SHARE, HALF), bf16),
            pltpu.VMEM((NDP, 3, COLD_SHARE, HALF), bf16),
            dma((5,)),
            dma((6,)),
            dma((2, NDP)),
            dma((2, NDP)),
            dma((2, NX)),
            dma((2, NX)),
            dma((2, NDP)),
            dma((2, CHUNKS, NY - 1)),
            dma((2, CHUNKS, NY - 1)),
            dma((NZ,)),
            dma((NZ,)),
            dma((len(FAR),)),
            dma((NDP,)),
            dma((NDP,)),
            pltpu.SemaphoreType.REGULAR((2,)),
        ],
        compiler_params=pltpu.CompilerParams(collective_id=0, has_side_effects=True, vmem_limit_bytes=32 * 1024 * 1024),
    )(*(pltpu.with_memory_space_constraint(a, pltpu.HBM) for a in operands))
    return pl.pallas_call(
        adam_kernel,
        name="adam",
        out_shape=shapes,
        in_specs=[smem] + [vmem] * 7,
        out_specs=[hbm] * 6,
        scratch_shapes=[pltpu.VMEM(a.shape, a.dtype) for a in state] + [dma((3, 3))],
    )(live_rows, *(pltpu.with_memory_space_constraint(a, pltpu.VMEM) for a in staged))


def solution(mesh):
    rows = P(("dp", "table"), None)
    shard = P("table", None)
    return jax.shard_map(
        per_device, mesh=mesh, in_specs=(rows,) * 4 + (P("table"),) + (shard,) * 6, out_specs=(shard,) * 6,
        check_vma=False)
```

time: 49.8 us -> 45.6 us (0.916)
  Pallas kernels: 48.3 us -> 44.1 us
    pallas_call x2, Pallas kernels: 48.3 us -> 44.1 us  [the longest x1 42.9 us: per_device(): pl.pallas_call(comm_kernel, name='gradients', out_shape=[jax.ShapeDtypeSt...]
where the time goes in v3:
time: 45.6 us; the launch traced here: 45.4 us
  Pallas kernels  44.1 us (97%)
  between operations  1.29 us (3%)
    pallas_call x1, Pallas kernels, per_device(): pl.pallas_call(comm_kernel, name='gradients', out_shape=[jax.ShapeDtypeSt...  42.9 us
    pallas_call x1, Pallas kernels, per_device(): pl.pallas_call(adam_kernel, name='adam', out_shape=shapes, in_specs=[smem...  1.24 us

profile of v3, /device:TPU:1, one launch (start us, length us, event | category | flops | bytes accessed | tf_op | source)
XLA Modules:
  0.0 45.4 jit_solution(2654085786755648138)
XLA Ops:
  1.3 42.9 %gradients.1 = (bf16[8,3,16,128]{3,2,1,0:T(8,128)(2,1)S(1)}, f32[32,256]{1,0:T(8,128)S(1)}, f32[32,256]{1,0:T(8,128)S(1)}, f32[32,256]{1,0:T(8,128)S(1)}, f32[25...) custom-call(bf16[256,256]{1,0:T(8,128)(2,1)} %cot_hbm.1, s32[8,256]{1,0:T(8,128)} %bitcast.3, ...), custom_call_target="tpu_custom_call" | custom-call | tf_op jit(solution)/shard_map/gradients/pallas_call | solution.py:350
  44.2 1.2 %adam.1 = (f32[32,256]{1,0:T(8,128)}, f32[32,256]{1,0:T(8,128)}, f32[32,256]{1,0:T(8,128)}, f32[256,256]{1,0:T(8,128)}, f32[256,256]{1,0:T(8,128)}, /*index=5*/f32[256,256]{1,0:T(8,128)}) custom-call(s32[1]{0:T(128)S(6)} %copy.17.live, bf16[8,3,16,128]{3,2,1,0:T(8,128)(2,1)S(1)} %get-tuple-element.13.grads, f32[32,256]{1,0:T(8,128)S(1)} %get-tuple-element.14.refs_0_, ...), custom_call_target="tpu_custom_call" | custom-call | tf_op jit(solution)/shard_map/adam/pallas_call | solution.py:393

commit v4 on v3

--- a/solution.py
+++ b/solution.py
@@ -91,8 +91,6 @@
         pltpu.make_async_copy(a, b, state_sem.at[i])
         for i, (a, b) in enumerate(zip((s0, s1, s2, s3, s4, s5), (o0, o1, o2, o3, o4, o5)))
     ]
-    for cp in states:
-        cp.start()
 
     row = lax.broadcasted_iota(jnp.int32, (NY * NZ, SAMP), 0)
     order = (row // (NY * PER)) * PER + row % PER
@@ -201,23 +199,28 @@
 
         lax.fori_loop(1, NX, build_other, 0)
 
-    for k in (1, 3, 2):
+    for k in (2, 1, 3):
         for h in range(2):
             arrive(cot.at[h, k], cot_recv.at[h, k])
             forward(h, k)
-
-    middle = NX * SAMP
-    for h in range(2):
-        mine = cot[h, 0:NX].reshape(middle, HALF)
-        for q in range(CHUNKS):
-            part[h, q] = jnp.dot(counts[h, q, :, 0:middle], mine, preferred_element_type=jnp.float32)
-    for h in range(2):
-        for k in (0, 1, 3, 2):
+    for cp in states:
+        cp.start()
+
+    def product(h, q, first):
+        left = counts[h, q, :, first * SAMP:(first + NX) * SAMP]
+        right = cot[h, first:first + NX].reshape(NX * SAMP, HALF)
+        return jnp.dot(left, right, preferred_element_type=jnp.float32)
+
+    ahead = 2
+    for q in range(ahead):
+        for h in range(2):
+            part[h, q] = product(h, q, 0)
+    for k in (0, 2, 1, 3):
+        for h in range(2):
             arrive(cot.at[h, NX + k], cot_recv.at[h, NX + k])
     for q in range(CHUNKS):
         for h in range(2):
-            others = cot[h, NX:NDP].reshape(middle, HALF)
-            done = part[h, q] + jnp.dot(counts[h, q, :, middle:2 * middle], others, preferred_element_type=jnp.float32)
+            done = (part[h, q] if q < ahead else product(h, q, 0)) + product(h, q, NX)
             psum_own[h, q] = done[0:BLOCK]
             for r in (2, 1, 3):
                 rsend[h, q, r - 1] = done[r * BLOCK:(r + 1) * BLOCK].astype(jnp.bfloat16)

time: 45.6 us -> 45.4 us (level)
  no operation moved by 1% of the time
where the time goes in v4:
time: 45.4 us; the launch traced here: 45.2 us
  Pallas kernels  43.9 us (97%)
  between operations  1.29 us (3%)
    pallas_call x1, Pallas kernels, per_device(): pl.pallas_call(comm_kernel, name='gradients', out_shape=[jax.ShapeDtypeSt...  42.7 us
    pallas_call x1, Pallas kernels, per_device(): pl.pallas_call(adam_kernel, name='adam', out_shape=shapes, in_specs=[smem...  1.24 us

profile of v4, /device:TPU:1, one launch (start us, length us, event | category | flops | bytes accessed | tf_op | source)
XLA Modules:
  0.0 45.2 jit_solution(1718887958783066272)
XLA Ops:
  1.3 42.7 %gradients.1 = (bf16[8,3,16,128]{3,2,1,0:T(8,128)(2,1)S(1)}, f32[32,256]{1,0:T(8,128)S(1)}, f32[32,256]{1,0:T(8,128)S(1)}, f32[32,256]{1,0:T(8,128)S(1)}, f32[25...) custom-call(bf16[256,256]{1,0:T(8,128)(2,1)} %cot_hbm.1, s32[8,256]{1,0:T(8,128)} %bitcast.3, ...), custom_call_target="tpu_custom_call" | custom-call | tf_op jit(solution)/shard_map/gradients/pallas_call | solution.py:353
  44.0 1.2 %adam.1 = (f32[32,256]{1,0:T(8,128)}, f32[32,256]{1,0:T(8,128)}, f32[32,256]{1,0:T(8,128)}, f32[256,256]{1,0:T(8,128)}, f32[256,256]{1,0:T(8,128)}, /*index=5*/f32[256,256]{1,0:T(8,128)}) custom-call(s32[1]{0:T(128)S(6)} %copy.17.live, bf16[8,3,16,128]{3,2,1,0:T(8,128)(2,1)S(1)} %get-tuple-element.13.grads, f32[32,256]{1,0:T(8,128)S(1)} %get-tuple-element.14.refs_0_, ...), custom_call_target="tpu_custom_call" | custom-call | tf_op jit(solution)/shard_map/adam/pallas_call | solution.py:396

commit v5 on v3

--- a/solution.py
+++ b/solution.py
@@ -91,8 +91,6 @@
         pltpu.make_async_copy(a, b, state_sem.at[i])
         for i, (a, b) in enumerate(zip((s0, s1, s2, s3, s4, s5), (o0, o1, o2, o3, o4, o5)))
     ]
-    for cp in states:
-        cp.start()
 
     row = lax.broadcasted_iota(jnp.int32, (NY * NZ, SAMP), 0)
     order = (row // (NY * PER)) * PER + row % PER
@@ -205,6 +203,8 @@
         for h in range(2):
             arrive(cot.at[h, k], cot_recv.at[h, k])
             forward(h, k)
+    for cp in states:
+        cp.start()
 
     middle = NX * SAMP
     for h in range(2):

time: 45.6 us -> 45.5 us (level)
  no operation moved by 1% of the time
where the time goes in v5:
time: 45.5 us; the launch traced here: 45.4 us
  Pallas kernels  44.1 us (97%)
  between operations  1.29 us (3%)
    pallas_call x1, Pallas kernels, per_device(): pl.pallas_call(comm_kernel, name='gradients', out_shape=[jax.ShapeDtypeSt...  42.8 us
    pallas_call x1, Pallas kernels, per_device(): pl.pallas_call(adam_kernel, name='adam', out_shape=shapes, in_specs=[smem...  1.24 us

profile of v5, /device:TPU:1, one launch (start us, length us, event | category | flops | bytes accessed | tf_op | source)
XLA Modules:
  0.0 45.4 jit_solution(9597634134938661489)
XLA Ops:
  1.3 42.8 %gradients.1 = (bf16[8,3,16,128]{3,2,1,0:T(8,128)(2,1)S(1)}, f32[32,256]{1,0:T(8,128)S(1)}, f32[32,256]{1,0:T(8,128)S(1)}, f32[32,256]{1,0:T(8,128)S(1)}, f32[25...) custom-call(bf16[256,256]{1,0:T(8,128)(2,1)} %cot_hbm.1, s32[8,256]{1,0:T(8,128)} %bitcast.3, ...), custom_call_target="tpu_custom_call" | custom-call | tf_op jit(solution)/shard_map/gradients/pallas_call | solution.py:350
  44.1 1.2 %adam.1 = (f32[32,256]{1,0:T(8,128)}, f32[32,256]{1,0:T(8,128)}, f32[32,256]{1,0:T(8,128)}, f32[256,256]{1,0:T(8,128)}, f32[256,256]{1,0:T(8,128)}, /*index=5*/f32[256,256]{1,0:T(8,128)}) custom-call(s32[1]{0:T(128)S(6)} %copy.17.live, bf16[8,3,16,128]{3,2,1,0:T(8,128)(2,1)S(1)} %get-tuple-element.13.grads, f32[32,256]{1,0:T(8,128)S(1)} %get-tuple-element.14.refs_0_, ...), custom_call_target="tpu_custom_call" | custom-call | tf_op jit(solution)/shard_map/adam/pallas_call | solution.py:393
